TPU v7x, 32 devices: a whole 2x2x4 slice. The times are simulated.
32 devices in a mesh: blk: 4 (over z), group: 8 (over y, x, core).
Axes of the slice: x: 2, y: 2, z: 4, core: 2. Of those that a mesh axis runs over, the one named last changes fastest.
Arguments:
- positions: float32 [3, 262144], P(None, ('blk', 'group')), may hold values from -6 to 6
- velocities: float32 [3, 262144], P(None, ('blk', 'group')), may hold values from -6 to 6
- accelerations: float32 [3, 262144], P(None, ('blk', 'group')), may hold values from -6 to 6
- jerk_rates: float32 [3, 262144], P(None, ('blk', 'group')), may hold values from -24 to 24
- masses: float32 [262144], P(('blk', 'group')), may hold values from 0.1 to 10
- elapsed_time: float32 [262144], P(('blk', 'group')), may hold values from 0.05 to 0.5
- active_index: int32 [512], P(('blk', 'group')), may hold values from 0 to 262143
Outputs:
- new_pos: float32 [3, 512], P(None, ('blk', 'group'))
- new_vel: float32 [3, 512], P(None, ('blk', 'group'))
- new_acc: float32 [3, 512], P(None, ('blk', 'group'))
- new_jerk: float32 [3, 512], P(None, ('blk', 'group'))
All inputs are finite; a program needn't handle non-finite values.
Results may differ from a plain program's by a relative error of at most 0.0003.
Values sent between devices are 32-bit elements; how exact they have to be, the bound alone decides.
A program may use at most 128 MiB of HBM per device.

v0:
```python
import math

import jax
import jax.numpy as jnp
from jax import lax
from jax.sharding import PartitionSpec as P

softening = 0.001


def predict(pos_now, vel_now, acc_now, jerk_now, elapsed):
    pred_pos = pos_now + elapsed * (
        vel_now + elapsed * (0.5 * acc_now + elapsed * (jerk_now / 6.0))
    )
    pred_vel = vel_now + elapsed * (acc_now + elapsed * (0.5 * jerk_now))
    return (pred_pos, pred_vel)


def block_forces(active_data, field_piece):
    offset = field_piece[0:3, None, :] - active_data[0:3, :, None]
    motion = field_piece[3:6, None, :] - active_data[3:6, :, None]
    dist_sq = jnp.sum(offset * offset, axis=0) + softening
    inverse = lax.rsqrt(dist_sq)
    weight = field_piece[6][None, :] * inverse * inverse * inverse
    factor = 3.0 * jnp.sum(offset * motion, axis=0) / dist_sq
    accel_part = jnp.sum(offset * weight, axis=2)
    jerk_part = jnp.sum((motion - factor * offset) * weight, axis=2)
    return jnp.concatenate([accel_part, jerk_part], axis=0)


def pair_forces(active_data, field):
    num_active = active_data.shape[1]
    num_field = field.shape[1]
    columns = math.gcd(num_field, max(1, 524288 // num_active))

    def advance(summed, which):
        field_piece = lax.dynamic_slice_in_dim(field, which * columns, columns, 1)
        return (summed + block_forces(active_data, field_piece), None)

    summed, _ = lax.scan(
        advance,
        jnp.zeros((6, num_active), jnp.float32),
        jnp.arange(num_field // columns, dtype=jnp.int32),
    )
    return summed


def corrector(owner_rows, forces):
    old_pos = owner_rows[0:3]
    old_vel = owner_rows[3:6]
    old_acc = owner_rows[6:9]
    old_jerk = owner_rows[9:12]
    elapsed = owner_rows[12]
    new_acc = forces[0:3]
    new_jerk = forces[3:6]
    squared = elapsed * elapsed / 12.0
    new_vel = old_vel + 0.5 * elapsed * (old_acc + new_acc) + squared * (old_jerk - new_jerk)
    new_pos = old_pos + 0.5 * elapsed * (old_vel + new_vel) + squared * (old_acc - new_acc)
    return (new_pos, new_vel, new_acc, new_jerk)


def on_device(positions, velocities, accelerations, jerk_rates, masses, elapsed_time, active_index):
    own_stars = positions.shape[1]
    total_stars = own_stars * lax.axis_size("blk") * lax.axis_size("group")
    gravity = 1.0 / total_stars
    pred_pos, pred_vel = predict(positions, velocities, accelerations, jerk_rates, elapsed_time)
    own_field = jnp.concatenate([pred_pos, pred_vel, masses[None, :]], axis=0)
    packed = jnp.concatenate(
        [positions, velocities, accelerations, jerk_rates, elapsed_time[None, :]], axis=0
    )
    every_index = lax.all_gather(active_index, ("blk", "group"), axis=0, tiled=True)
    first_row = lax.axis_index(("blk", "group")) * own_stars
    local_row = every_index - first_row
    is_owned = (local_row >= 0) & (local_row < own_stars)
    picked = jnp.take(packed, jnp.clip(local_row, 0, own_stars - 1), axis=1)
    picked = picked * is_owned.astype(jnp.float32)[None, :]
    owner_rows = lax.psum_scatter(picked, ("blk", "group"), scatter_dimension=1, tiled=True)
    mine_pos, mine_vel = predict(
        owner_rows[0:3], owner_rows[3:6], owner_rows[6:9], owner_rows[9:12], owner_rows[12]
    )
    mine_state = jnp.concatenate([mine_pos, mine_vel], axis=0)
    field_group = lax.all_gather(own_field, "group", axis=1, tiled=True)
    group_state = lax.all_gather(mine_state, "blk", axis=1, tiled=True)
    partial_sum = pair_forces(group_state, field_group)
    forces = lax.psum_scatter(partial_sum, "blk", scatter_dimension=1, tiled=True)
    return corrector(owner_rows, forces * gravity)


def solution(mesh):
    return jax.shard_map(
        on_device,
        mesh=mesh,
        in_specs=(
            P(None, ("blk", "group")),
            P(None, ("blk", "group")),
            P(None, ("blk", "group")),
            P(None, ("blk", "group")),
            P(("blk", "group")),
            P(("blk", "group")),
            P(("blk", "group")),
        ),
        out_specs=(
            P(None, ("blk", "group")),
            P(None, ("blk", "group")),
            P(None, ("blk", "group")),
            P(None, ("blk", "group")),
        ),
        check_vma=False,
    )
```

profile of v0, /device:TPU:0, one launch (start us, length us, event | category | flops | bytes accessed | tf_op | source)
XLA Modules:
  0.0 325.5 jit_solution(5370106172625090832)
XLA Ops:
  9.1 42.0 %all-reduce = s32[512]{0:T(512)S(1)} all-reduce(s32[512]{0:T(512)S(1)} %dynamic-update-slice), channel_id=1, replica_groups=mesh['blk'=4,'group'=8] {'blk','group'}, use_global_device_ids=true, to_apply=%add | all-reduce | flops 512 | bytes 4096
  51.1 4.0 %concatenate.12 = f32[13,8192]{1,0:T(8,128)S(1)} concatenate(f32[3,8192]{1,0:T(4,128)} %param.9, f32[3,8192]{1,0:T(4,128)} %param.10, f32[3,8192]{1,0:T(4,128)} %param.11, f32[3,8192]{1,0:T(4,128)} %param.12, f32[1,8192]{1,0:T(1,128)} %bitcast.17), dimensions={0} | concatenate | bytes 851968 | tf_op jit(solution)/shard_map/concatenate | solution.py:68
  55.2 2.6 copy.41
  57.8 3.2 gather_fusion
  63.1 132.7 %reduce-scatter.3.cloned.1.call-done = f32[13,16]{0,1:T(8,128)} async-done(((f32[13,512]{0,1:T(8,128)}), f32[13,16]{0,1:T(8,128)}) %reduce-scatter.3.cloned.1.call-update) | async-done | bytes 848 | tf_op jit(solution)/shard_map/reduce_scatter | solution.py:77
  197.8 13.1 %all-gather = f32[4,16,6]{1,2,0:T(8,128)S(1)} all-gather(f32[1,16,6]{1,2,0:T(8,128)S(1)} %bitcast.20), channel_id=1, replica_groups=mesh['blk'=4,'group'=8] {'blk'}, dimensions={0}, use_global_device_ids=true | all-gather | bytes 1920 | tf_op jit(solution)/shard_map/all_gather | solution.py:83
  211.0 87.5 %while.11 = (s32[]{:T(128)}, f32[6,64]{1,0:T(8,128)S(1)}, s32[8]{0:T(128)S(1)}, f32[7,65536]{1,0:T(8,128)}, f32[6,64]{1,0:T(8,128)S(1)}, /*index=5*/s32[]{:T(128...) while((s32[]{:T(128)}, f32[6,64]{1,0:T(8,128)S(1)}, s32[8]{0:T(128)S(1)}, ...), condition=%wide.region_6.7_spmd.clone, body=%wide.region_1.6_spmd.clone.sunk | while | flops 24118024 | bytes 17674452 | solution.py:40
  213.4 3.0 fusion.13
  217.5 2.1 multiply_divide_fusion.2
  219.7 2.2 fusion.14
  224.4 3.0 fusion.13
  228.5 2.1 multiply_divide_fusion.2
  230.6 2.2 fusion.14
  235.3 3.0 fusion.13
  239.4 2.1 multiply_divide_fusion.2
  241.6 2.2 fusion.14
  246.3 3.0 fusion.13
  250.4 2.1 multiply_divide_fusion.2
  252.5 2.2 fusion.14
  257.2 3.0 fusion.13
  261.3 2.1 multiply_divide_fusion.2
  263.4 2.2 fusion.14
  268.1 3.0 fusion.13
  272.2 2.1 multiply_divide_fusion.2
  274.4 2.2 fusion.14
  279.1 3.0 fusion.13
  283.2 2.1 multiply_divide_fusion.2
  285.3 2.2 fusion.14
  290.0 3.0 fusion.13
  294.1 2.1 multiply_divide_fusion.2
  296.3 2.2 fusion.14
  299.3 15.4 %reduce-scatter.5.cloned.1.call-done = f32[6,16]{0,1:T(8,128)} async-done(((f32[6,64]{0,1:T(8,128)}), f32[6,16]{0,1:T(8,128)}) %reduce-scatter.5.cloned.1.call-update) | async-done | bytes 400 | tf_op jit(solution)/shard_map/reduce_scatter | solution.py:85
  (85 shorter events, 32.0 us)
Async XLA Ops:
  8.0 54.0 %copy-start.5 = (f32[8192]{0:T(1024)S(1)}, f32[8192]{0:T(1024)}, u32[]{:S(2)}) copy-start(f32[8192]{0:T(1024)} %param.14) | copy-start | bytes 98308
  8.0 54.1 %copy-start.2 = (f32[3,8192]{1,0:T(4,128)S(1)}, f32[3,8192]{1,0:T(4,128)}, u32[]{:S(2)}) copy-start(f32[3,8192]{1,0:T(4,128)} %param.10) | copy-start | bytes 294916
  8.0 54.0 %copy-start.3 = (f32[3,8192]{1,0:T(4,128)S(1)}, f32[3,8192]{1,0:T(4,128)}, u32[]{:S(2)}) copy-start(f32[3,8192]{1,0:T(4,128)} %param.11) | copy-start | bytes 294916
  8.0 54.0 %copy-start.4 = (f32[3,8192]{1,0:T(4,128)S(1)}, f32[3,8192]{1,0:T(4,128)}, u32[]{:S(2)}) copy-start(f32[3,8192]{1,0:T(4,128)} %param.12) | copy-start | bytes 294916
  8.0 54.0 %copy-start.1 = (f32[3,8192]{1,0:T(4,128)S(1)}, f32[3,8192]{1,0:T(4,128)}, u32[]{:S(2)}) copy-start(f32[3,8192]{1,0:T(4,128)} %param.9) | copy-start | bytes 294916
  8.1 54.2 %copy-start.6 = (f32[8192]{0:T(1024)S(1)}, f32[8192]{0:T(1024)}, u32[]{:S(2)}) copy-start(f32[8192]{0:T(1024)} %param.13) | copy-start | bytes 98308
  8.1 187.7 %reduce-scatter.3.cloned.1.call-start = ((), (), s32[]{:S(2)}) async-start(), calls=%async_computation.2 | async-start | bytes 270336 | tf_op jit(solution)/shard_map/reduce_scatter | solution.py:77
  62.0 149.0 %all-gather.3.cloned.1.call-start = ((), (), s32[]{:S(2)}) async-start(), calls=%async_computation.3 | async-start | bytes 2359296 | tf_op jit(solution)/shard_map/all_gather | solution.py:82
  63.1 251.6 %reduce-scatter.5.cloned.1.call-start = ((), (), s32[]{:S(2)}) async-start(), calls=%async_computation.4 | async-start | bytes 40960 | tf_op jit(solution)/shard_map/reduce_scatter | solution.py:85
  211.0 104.3 %copy-start = (f32[13,16]{0,1:T(8,128)S(1)}, f32[13,16]{0,1:T(8,128)}, u32[]{:S(2)}) copy-start(f32[13,16]{0,1:T(8,128)} %reduce-scatter.3.cloned.1.call-done) | copy-start | bytes 2500
Sparse Core Ops, SparseCore 0:
  62.1 133.6 reduce-scatter.2
  299.4 15.2 reduce-scatter.4
Sparse Core Ops, SparseCore 1:
  64.5 27.6 all-gather.2
where the time goes:
time: 327 us; the launch traced here: 325 us
  waiting for transfers between devices  148 us (45%)
  other arithmetic  63.9 us (20%)
  blocking collectives  55.1 us (17%)
  local copies, waits for them, and re-layouts  37 us (11%)
  between operations  15.7 us (5%)
  loops' own time  5.56 us (2%)
    reduce_scatter x1, waiting for transfers between devices, on_device(): lax.psum_scatter(picked, ('blk', 'group'), scatter_dimension=1, tiled=True)  133 us
    unnamed x1, blocking collectives  42 us
    reduce_sum x8, other arithmetic, block_forces(): dist_sq = jnp.sum(offset * offset, axis=0) + softening  24.1 us
    reduce_sum x8, other arithmetic, block_forces(): accel_part = jnp.sum(offset * weight, axis=2)  18 us
    div x8, other arithmetic, block_forces(): factor = 3.0 * jnp.sum(offset * motion, axis=0) / dist_sq  17.2 us
    reduce_scatter x1, waiting for transfers between devices, on_device(): lax.psum_scatter(partial_sum, 'blk', scatter_dimension=1, tiled=True)  15.4 us
    all_gather x1, blocking collectives, on_device(): group_state = lax.all_gather(mine_state, 'blk', axis=1, tiled=True)  13.1 us
    slice x16, local copies, waits for them, and re-layouts, block_forces(): motion = field_piece[3:6, None, :] - active_data[3:6, :, None]  9.34 us
  transfers between devices with their start and end apart: 3, of which 2 were waited for; matrix products, arithmetic and copies ran while one was open for 1% of the time, Pallas kernels for 0%

commit v1 on v0

v1 whole, which is shorter than its diff:
```python
import functools

import jax
import jax.numpy as jnp
from jax import lax
from jax.experimental import pallas as pl
from jax.experimental.pallas import tpu as pltpu
from jax.sharding import PartitionSpec as P

softening = 0.001
MESH = pl.DeviceIdType.MESH
F32 = jnp.float32
BF16 = jnp.bfloat16
LANES = 128
CHUNK = 256
ROWS = 512
PARTS = ((0, 0), (0, 1), (1, 0), (0, 2), (2, 0), (1, 1))
NT = (((1,), (1,)), ((), ()))


def predict(pos_now, vel_now, acc_now, jerk_now, elapsed):
    pred_pos = pos_now + elapsed * (
        vel_now + elapsed * (0.5 * acc_now + elapsed * (jerk_now / 6.0))
    )
    pred_vel = vel_now + elapsed * (acc_now + elapsed * (0.5 * jerk_now))
    return (pred_pos, pred_vel)


def split3(value):
    high = value.astype(BF16).astype(F32)
    rest = value - high
    middle = rest.astype(BF16).astype(F32)
    low = (rest - middle).astype(BF16).astype(F32)
    return (high, middle, low)


def padded(pieces, rows):
    have = sum(piece.shape[0] for piece in pieces)
    width = pieces[0].shape[1]
    if have < rows:
        pieces = list(pieces) + [jnp.zeros((rows - have, width), F32)]
    return jnp.concatenate(pieces, axis=0)


def kernel(
    blocks, groups, total_stars,
    pos_ref, vel_ref, acc_ref, jerk_ref, mass_ref, time_ref, index_ref,
    out_pos, out_vel, out_acc, out_jerk,
    index_all, index_col, packed, field_u, field_s, motion_rhs, field_pos,
    picked, send_state, recv_state, state_all, state, rows_lhs, rows_pos,
    weights_a, weights_b, sums, send_force, recv_force,
    send_sem, recv_sem,
):
    devices = blocks * groups
    own_stars = pos_ref.shape[1]
    own_active = index_ref.shape[1]
    active = devices * own_active
    lane_blocks = active // LANES
    per_block = LANES // own_active
    me = lax.axis_index("blk") * groups + lax.axis_index("group")

    def peer_of(step):
        peer = lax.rem(me + step, devices)
        return peer, (peer // groups, lax.rem(peer, groups))

    barrier = pltpu.get_barrier_semaphore()

    def greet(step, carry):
        pl.semaphore_signal(barrier, inc=1, device_id=peer_of(step)[1], device_id_type=MESH)
        return carry

    lax.fori_loop(1, devices, greet, 0)

    def exchange(phase, source, target):
        def copy_to(step):
            peer, where = peer_of(step)
            return pltpu.make_async_remote_copy(
                src_ref=source(peer),
                dst_ref=target.at[me],
                send_sem=send_sem.at[phase, step],
                recv_sem=recv_sem.at[phase, me],
                device_id=where,
                device_id_type=MESH,
            )

        def start(step, carry):
            copy_to(step).start()
            return carry

        def finish(step, carry):
            sender = lax.rem(me + step, devices)
            pltpu.make_async_remote_copy(
                src_ref=source(sender),
                dst_ref=target.at[sender],
                send_sem=send_sem.at[phase, step],
                recv_sem=recv_sem.at[phase, sender],
                device_id=peer_of(step)[1],
                device_id_type=MESH,
            ).wait()
            return carry

        lax.fori_loop(1, devices, start, 0)
        return lambda: lax.fori_loop(1, devices, finish, 0)

    index_row = jnp.concatenate(
        [index_ref[...], jnp.zeros((1, LANES - own_active), jnp.int32)], axis=1
    )
    index_all[me] = index_row
    pl.semaphore_wait(barrier, devices - 1)
    finish_index = exchange(0, lambda peer: index_all.at[me], index_all)

    piece = 1024

    def prepare(which, carry):
        at = pl.ds(pl.multiple_of(which * piece, piece), piece)
        old_pos, old_vel, old_acc, old_jerk = (
            ref[:, at] for ref in (pos_ref, vel_ref, acc_ref, jerk_ref)
        )
        mass, elapsed = mass_ref[:, at], time_ref[:, at]
        pred_pos, pred_vel = predict(old_pos, old_vel, old_acc, old_jerk, elapsed)
        rows = padded([old_pos, old_vel, old_acc, old_jerk, elapsed], 16)
        packed[:, at] = padded(split3(rows), LANES).astype(BF16)
        field_pos[:, at] = padded([pred_pos], 8)
        moments = padded([mass * pred_pos, mass * pred_vel, mass], 8)
        split = jnp.concatenate(split3(moments), axis=0)
        field_u[:, at] = padded([split], LANES).astype(BF16)
        field_s[:, at] = padded([jnp.zeros((32, piece), F32), split], LANES).astype(BF16)
        pos_parts, vel_parts = split3(pred_pos), split3(pred_vel)
        dot_parts = split3(jnp.sum(pred_pos * pred_vel, axis=0, keepdims=True))
        ones = jnp.ones((1, piece), F32)
        rhs = [pos_parts[right] for _, right in PARTS] + [vel_parts[right] for _, right in PARTS]
        motion_rhs[:, at] = padded(rhs + list(dot_parts) + [ones] * 3, LANES).astype(BF16)
        return carry

    lax.fori_loop(0, own_stars // piece, prepare, 0)

    finish_index()
    first = me * own_stars
    local = (index_all[...].reshape(devices, LANES) - first).astype(F32)
    local = jnp.transpose(local)
    for device in range(devices):
        column = local[:own_active, device : device + 1]
        index_col[device * own_active : (device + 1) * own_active, :] = jnp.broadcast_to(
            column, (own_active, LANES)
        )

    wide = 512
    tile = min(ROWS, active)

    for block in range(active // tile):
        picked[block * tile : (block + 1) * tile, :] = jnp.zeros((tile, LANES), F32)

        def pick(which, carry):
            base = which * wide
            at = pl.ds(pl.multiple_of(base, wide), wide)
            lanes = lax.broadcasted_iota(jnp.int32, (1, wide), 1) + base
            lanes = lanes.astype(F32)
            pieces = []
            for part in range(wide // LANES):
                column = index_col[block * tile : (block + 1) * tile, :]
                same = column == lanes[:, part * LANES : (part + 1) * LANES]
                pieces.append(jnp.where(same, 1.0, 0.0).astype(BF16))
            chosen = jnp.concatenate(pieces, axis=1)
            picked[block * tile : (block + 1) * tile, :] += lax.dot_general(
                chosen, packed[:, at], NT, preferred_element_type=F32
            )
            return carry

        lax.fori_loop(0, own_stars // wide, pick, 0)

    for block in range(lane_blocks):
        turned = jnp.transpose(picked[block * LANES : (block + 1) * LANES, :])
        rows = turned[0:16] + turned[16:32] + turned[32:48]
        for pair in range(per_block):
            send_state[block * per_block + pair] = rows[2 * pair : 2 * pair + 2]
    recv_state[me] = send_state[me]
    exchange(1, lambda peer: send_state.at[peer], recv_state)()
    state_all[me] = jnp.sum(recv_state[...], axis=0)
    exchange(2, lambda peer: state_all.at[me], state_all)()

    for block in range(lane_blocks):
        for pair in range(per_block):
            state[block, 2 * pair : 2 * pair + 2, :] = state_all[block * per_block + pair]
    for block in range(lane_blocks):
        rows = state[block]
        pred_pos, pred_vel = predict(rows[0:3], rows[3:6], rows[6:9], rows[9:12], rows[12:13])
        pos_parts, vel_parts = split3(-pred_pos), split3(-pred_vel)
        dot_parts = split3(jnp.sum(pred_pos * pred_vel, axis=0, keepdims=True))
        ones = jnp.ones((1, LANES), F32)
        lhs = [vel_parts[left] for left, _ in PARTS] + [pos_parts[left] for left, _ in PARTS]
        lhs = jnp.transpose(padded(lhs + [ones] * 3 + list(dot_parts), LANES))
        rows_lhs[block * LANES : (block + 1) * LANES, :] = lhs.astype(BF16)
        columns = jnp.transpose(padded([pred_pos], LANES))
        for axis in range(3):
            rows_pos[axis, block * LANES : (block + 1) * LANES, :] = jnp.broadcast_to(
                columns[:, axis : axis + 1], (LANES, LANES)
            )

    chunks = own_stars // CHUNK

    def pair_weights(first_row, which, target):
        at = pl.ds(pl.multiple_of(which * CHUNK, CHUNK), CHUNK)
        stars = [field_pos[axis : axis + 1, at] for axis in range(3)]
        along = jnp.dot(
            rows_lhs[pl.ds(first_row, tile), :], motion_rhs[:, at], preferred_element_type=F32
        )
        high = 16
        for row in range(0, tile, high):
            mine = [rows_pos[axis, pl.ds(first_row + row, high), :] for axis in range(3)]
            for lane in range(0, CHUNK, LANES):
                squares = []
                for axis in range(3):
                    offset = stars[axis][:, lane : lane + LANES] - mine[axis]
                    squares.append(offset * offset)
                inverse = lax.rsqrt(squares[0] + squares[1] + squares[2] + softening)
                inverse_sq = inverse * inverse
                cubed = inverse_sq * inverse
                slope = cubed * (inverse_sq * along[row : row + high, lane : lane + LANES])
                for number, value in enumerate((cubed, slope)):
                    near = value.astype(BF16)
                    far = (value - near.astype(F32)).astype(BF16)
                    start = 2 * number * CHUNK + lane
                    target[row : row + high, start : start + LANES] = near
                    start += CHUNK
                    target[row : row + high, start : start + LANES] = far

    def add_up(first_row, which, source):
        at = pl.ds(pl.multiple_of(which * CHUNK, CHUNK), CHUNK)
        near, far = field_u[:, at], field_s[:, at]
        field = jnp.concatenate([near, near, far, far], axis=1)
        sums[pl.ds(first_row, tile), :] += lax.dot_general(
            source[...], field, NT, preferred_element_type=F32
        )

    for block in range(active // tile):
        first_row = block * tile
        sums[pl.ds(first_row, tile), :] = jnp.zeros((tile, LANES), F32)
        pair_weights(first_row, 0, weights_a)

        def advance(which, carry):
            pair_weights(first_row, 2 * which + 1, weights_b)
            add_up(first_row, 2 * which, weights_a)
            pair_weights(first_row, lax.rem(2 * which + 2, chunks), weights_a)
            add_up(first_row, 2 * which + 1, weights_b)
            return carry

        lax.fori_loop(0, chunks // 2, advance, 0)

    gravity = 1.0 / total_stars
    for block in range(lane_blocks):
        turned = jnp.transpose(sums[block * LANES : (block + 1) * LANES, :])
        plain = turned[0:8] + turned[8:16] + turned[16:24]
        sloped = turned[32:40] + turned[40:48] + turned[48:56]
        rows = state[block]
        pred_pos, pred_vel = predict(rows[0:3], rows[3:6], rows[6:9], rows[9:12], rows[12:13])
        accel = plain[0:3] - pred_pos * plain[6:7]
        jerk = (plain[3:6] - pred_vel * plain[6:7]) - 3.0 * (
            sloped[0:3] - pred_pos * sloped[6:7]
        )
        send_force[block] = padded([accel, jerk], 8)
    mine = me // per_block
    recv_force[me] = send_force[mine]
    exchange(3, lambda peer: send_force.at[peer // per_block], recv_force)()
    forces = jnp.sum(recv_force[...], axis=0) * gravity
    rows = state[mine]
    shift = lax.rem(LANES - own_active * lax.rem(me, per_block), LANES)
    forces = pltpu.roll(forces, shift, 1)
    rows = pltpu.roll(rows, shift, 1)
    new_acc, new_jerk = forces[0:3], forces[3:6]
    old_pos, old_vel, old_acc, old_jerk = rows[0:3], rows[3:6], rows[6:9], rows[9:12]
    elapsed = rows[12:13]
    squared = elapsed * elapsed / 12.0
    new_vel = old_vel + 0.5 * elapsed * (old_acc + new_acc) + squared * (old_jerk - new_jerk)
    new_pos = old_pos + 0.5 * elapsed * (old_vel + new_vel) + squared * (old_acc - new_acc)
    out_pos[...] = new_pos[:, :own_active]
    out_vel[...] = new_vel[:, :own_active]
    out_acc[...] = new_acc[:, :own_active]
    out_jerk[...] = new_jerk[:, :own_active]


def solution(mesh):
    blocks, groups = mesh.shape["blk"], mesh.shape["group"]
    devices = blocks * groups

    def on_device(positions, velocities, accelerations, jerk_rates, masses, elapsed_time, active_index):
        own_stars = positions.shape[1]
        own_active = active_index.shape[0]
        active = devices * own_active
        lane_blocks = active // LANES
        tile = min(ROWS, active)
        out = jax.ShapeDtypeStruct((3, own_active), F32)
        vmem = pl.BlockSpec(memory_space=pltpu.VMEM)
        return pl.pallas_call(
            functools.partial(kernel, blocks, groups, own_stars * devices),
            out_shape=(out,) * 4,
            in_specs=[vmem] * 7,
            out_specs=(vmem,) * 4,
            scratch_shapes=[
                pltpu.VMEM((devices, 1, LANES), jnp.int32),
                pltpu.VMEM((active, LANES), F32),
                pltpu.VMEM((LANES, own_stars), BF16),
                pltpu.VMEM((LANES, own_stars), BF16),
                pltpu.VMEM((LANES, own_stars), BF16),
                pltpu.VMEM((LANES, own_stars), BF16),
                pltpu.VMEM((8, own_stars), F32),
                pltpu.VMEM((active, LANES), F32),
                pltpu.VMEM((devices, 2, LANES), F32),
                pltpu.VMEM((devices, 2, LANES), F32),
                pltpu.VMEM((devices, 2, LANES), F32),
                pltpu.VMEM((lane_blocks, 16, LANES), F32),
                pltpu.VMEM((active, LANES), BF16),
                pltpu.VMEM((3, active, LANES), F32),
                pltpu.VMEM((tile, 4 * CHUNK), BF16),
                pltpu.VMEM((tile, 4 * CHUNK), BF16),
                pltpu.VMEM((active, LANES), F32),
                pltpu.VMEM((lane_blocks, 8, LANES), F32),
                pltpu.VMEM((devices, 8, LANES), F32),
                pltpu.SemaphoreType.DMA((4, devices)),
                pltpu.SemaphoreType.DMA((4, devices)),
            ],
            compiler_params=pltpu.CompilerParams(
                collective_id=0, has_side_effects=True, vmem_limit_bytes=40 * 1024 * 1024
            ),
            cost_estimate=pl.CostEstimate(
                flops=40 * active * own_stars, bytes_accessed=4 * 14 * own_stars,
                transcendentals=active * own_stars,
            ),
        )(
            positions, velocities, accelerations, jerk_rates,
            masses.reshape(1, own_stars), elapsed_time.reshape(1, own_stars),
            active_index.reshape(1, own_active),
        )

    wide = P(None, ("blk", "group"))
    flat = P(("blk", "group"))
    return jax.shard_map(
        on_device,
        mesh=mesh,
        in_specs=(wide, wide, wide, wide, flat, flat, flat),
        out_specs=(wide,) * 4,
        check_vma=False,
    )
```

time: 327 us -> 65.1 us (0.20)
  waiting for transfers between devices: 148 us -> 0 us
  other arithmetic: 63.9 us -> 0 us
  Pallas kernels: 0 us -> 56.1 us
  blocking collectives: 55.1 us -> 0 us
  local copies, waits for them, and re-layouts: 37 us -> 8.09 us
  between operations: 15.7 us -> 0.66 us
  loops' own time: 5.56 us -> 0 us
    reduce_scatter x2 -> x0, waiting for transfers between devices: 148 us -> none  [the longest x1 133 us: on_device(): lax.psum_scatter(picked, ('blk', 'group'), scatter_dimension=1, tiled=True)]
    pallas_call x0 -> x1, Pallas kernels: none -> 56.1 us  [on_device(): pl.pallas_call(functools.partial(kernel, blocks, groups, own_stars * devi...]
    reduce_sum x16 -> x0, other arithmetic: 42.1 us -> none  [the longest x8 24.1 us: block_forces(): dist_sq = jnp.sum(offset * offset, axis=0) + softening]
    unnamed x1 -> x0, blocking collectives: 42 us -> none
    slice x24 -> x0, local copies, waits for them, and re-layouts: 17.9 us -> none  [the longest x16 9.34 us: block_forces(): motion = field_piece[3:6, None, :] - active_data[3:6, :, None]]
    div x8 -> x0, other arithmetic: 17.2 us -> none  [block_forces(): factor = 3.0 * jnp.sum(offset * motion, axis=0) / dist_sq]
    all_gather x1 -> x0, blocking collectives: 13.1 us -> none  [on_device(): group_state = lax.all_gather(mine_state, 'blk', axis=1, tiled=True)]
    concatenate x2 -> x0, local copies, waits for them, and re-layouts: 6.67 us -> none  [on_device(): jnp.concatenate([positions, velocities, accelerations, jerk_rates, elapse...]
  transfers between devices with their start and end apart: 3 -> 0, of which waited for: 2 -> 0; matrix products, arithmetic and copies ran while one was open for 1% -> 0% of each run, Pallas kernels for 0% -> 0%
where the time goes in v1:
time: 65.1 us; the launch traced here: 64.8 us
  Pallas kernels  56.1 us (86%)
  local copies, waits for them, and re-layouts  8.09 us (12%)
  between operations  0.66 us (1%)
    pallas_call x1, Pallas kernels, on_device(): pl.pallas_call(functools.partial(kernel, blocks, groups, own_stars * devi...  56.1 us
    unnamed x18, local copies, waits for them, and re-layouts  8.09 us

profile of v1, /device:TPU:0, one launch (start us, length us, event | category | flops | bytes accessed | tf_op | source)
XLA Modules:
  0.0 64.8 jit_solution(11444588444044788199)
XLA Ops:
  0.6 0.0 copy-start.6
  0.6 0.6 copy-done.6
  1.3 0.0 copy-start
  1.3 0.9 %copy-done = f32[3,8192]{1,0:T(4,128)S(1)} copy-done((f32[3,8192]{1,0:T(4,128)S(1)}, f32[3,8192]{1,0:T(4,128)}, u32[]{:S(2)}) %copy-start) | copy-done | bytes 98328
  2.2 0.0 copy-start.1
  2.2 0.9 %copy-done.1 = f32[3,8192]{1,0:T(4,128)S(1)} copy-done((f32[3,8192]{1,0:T(4,128)S(1)}, f32[3,8192]{1,0:T(4,128)}, u32[]{:S(2)}) %copy-start.1) | copy-done | bytes 98328
  3.1 0.0 copy-start.2
  3.1 0.9 %copy-done.2 = f32[3,8192]{1,0:T(4,128)S(1)} copy-done((f32[3,8192]{1,0:T(4,128)S(1)}, f32[3,8192]{1,0:T(4,128)}, u32[]{:S(2)}) %copy-start.2) | copy-done | bytes 98328
  4.0 0.0 copy-start.3
  4.0 0.9 %copy-done.3 = f32[3,8192]{1,0:T(4,128)S(1)} copy-done((f32[3,8192]{1,0:T(4,128)S(1)}, f32[3,8192]{1,0:T(4,128)}, u32[]{:S(2)}) %copy-start.3) | copy-done | bytes 98328
  4.9 0.0 copy-start.4
  4.9 0.8 %copy-done.4 = f32[8192]{0:T(1024)S(1)} copy-done((f32[8192]{0:T(1024)S(1)}, f32[8192]{0:T(1024)}, u32[]{:S(2)}) %copy-start.4) | copy-done | bytes 32792
  5.7 0.0 copy-start.5
  5.7 0.8 %copy-done.5 = f32[8192]{0:T(1024)S(1)} copy-done((f32[8192]{0:T(1024)S(1)}, f32[8192]{0:T(1024)}, u32[]{:S(2)}) %copy-start.5) | copy-done | bytes 32792
  6.4 56.1 %shard_map.102 = (f32[3,16]{1,0:T(4,128)S(1)}, f32[3,16]{1,0:T(4,128)S(1)}, f32[3,16]{1,0:T(4,128)S(1)}, f32[3,16]{1,0:T(4,128)S(1)}) custom-call(f32[3,8192]{1,0:T(4,128)S(1)} %copy-done, f32[3,8192]{1,0:T(4,128)S(1)} %copy-done.1, f32[3,8192]{1,0:T(4,128)S(1)} %copy-done.2, f32[3,8192]{1,0:T(4,128)S(1)} %copy-done.3, f32[1,8192]{1,0:T(1,128)S(1)} %bitcast.3, ...), custom_call_target="tpu_custom_call" | custom-call | flops 167772160 | bytes 458752 | tf_op jit(solution)/shard_map/pallas_call | solution.py:293
  62.5 0.6 copy.15
  63.1 0.6 copy.16
  63.6 0.6 copy.17
  64.2 0.6 copy.18
Async XLA Ops:
  0.6 0.7 %copy-start.6 = (s32[16]{0:T(128)S(1)}, s32[16]{0:T(128)}, u32[]{:S(2)}) copy-start(s32[16]{0:T(128)} %param.13) | copy-start | bytes 196
  1.3 0.9 %copy-start = (f32[3,8192]{1,0:T(4,128)S(1)}, f32[3,8192]{1,0:T(4,128)}, u32[]{:S(2)}) copy-start(f32[3,8192]{1,0:T(4,128)} %pos_ref.1) | copy-start | bytes 294916
  2.2 0.9 %copy-start.1 = (f32[3,8192]{1,0:T(4,128)S(1)}, f32[3,8192]{1,0:T(4,128)}, u32[]{:S(2)}) copy-start(f32[3,8192]{1,0:T(4,128)} %vel_ref.1) | copy-start | bytes 294916
  3.1 0.9 %copy-start.2 = (f32[3,8192]{1,0:T(4,128)S(1)}, f32[3,8192]{1,0:T(4,128)}, u32[]{:S(2)}) copy-start(f32[3,8192]{1,0:T(4,128)} %acc_ref.1) | copy-start | bytes 294916
  4.0 0.9 %copy-start.3 = (f32[3,8192]{1,0:T(4,128)S(1)}, f32[3,8192]{1,0:T(4,128)}, u32[]{:S(2)}) copy-start(f32[3,8192]{1,0:T(4,128)} %jerk_ref.1) | copy-start | bytes 294916
  4.9 0.8 %copy-start.4 = (f32[8192]{0:T(1024)S(1)}, f32[8192]{0:T(1024)}, u32[]{:S(2)}) copy-start(f32[8192]{0:T(1024)} %param.11) | copy-start | bytes 98308
  5.7 0.8 %copy-start.5 = (f32[8192]{0:T(1024)S(1)}, f32[8192]{0:T(1024)}, u32[]{:S(2)}) copy-start(f32[8192]{0:T(1024)} %param.12) | copy-start | bytes 98308

commit v2 on v1

--- a/solution.py
+++ b/solution.py
@@ -12,7 +12,8 @@
 F32 = jnp.float32
 BF16 = jnp.bfloat16
 LANES = 128
-CHUNK = 256
+CHUNK = 512
+DEEP = 64
 ROWS = 512
 PARTS = ((0, 0), (0, 1), (1, 0), (0, 2), (2, 0), (1, 1))
 NT = (((1,), (1,)), ((), ()))
@@ -44,13 +45,23 @@
 
 def kernel(
     blocks, groups, total_stars,
+    pos_hbm, vel_hbm, acc_hbm, jerk_hbm, mass_hbm, time_hbm, index_hbm,
+    result,
     pos_ref, vel_ref, acc_ref, jerk_ref, mass_ref, time_ref, index_ref,
-    out_pos, out_vel, out_acc, out_jerk,
     index_all, index_col, packed, field_u, field_s, motion_rhs, field_pos,
     picked, send_state, recv_state, state_all, state, rows_lhs, rows_pos,
     weights_a, weights_b, sums, send_force, recv_force,
-    send_sem, recv_sem,
+    send_sem, recv_sem, load_sem,
 ):
+    loads = [
+        pltpu.make_async_copy(far, near, load_sem.at[number])
+        for number, (far, near) in enumerate((
+            (index_hbm, index_ref), (pos_hbm, pos_ref), (vel_hbm, vel_ref), (acc_hbm, acc_ref),
+            (jerk_hbm, jerk_ref), (mass_hbm, mass_ref), (time_hbm, time_ref),
+        ))
+    ]
+    for load in loads:
+        load.start()
     devices = blocks * groups
     own_stars = pos_ref.shape[1]
     own_active = index_ref.shape[1]
@@ -69,39 +80,31 @@
         pl.semaphore_signal(barrier, inc=1, device_id=peer_of(step)[1], device_id_type=MESH)
         return carry
 
-    lax.fori_loop(1, devices, greet, 0)
+    lax.fori_loop(1, devices, greet, 0, unroll=True)
 
     def exchange(phase, source, target):
-        def copy_to(step):
+        def start(step, carry):
             peer, where = peer_of(step)
-            return pltpu.make_async_remote_copy(
+            pltpu.make_async_remote_copy(
                 src_ref=source(peer),
                 dst_ref=target.at[me],
-                send_sem=send_sem.at[phase, step],
-                recv_sem=recv_sem.at[phase, me],
+                send_sem=send_sem.at[phase],
+                recv_sem=recv_sem.at[phase],
                 device_id=where,
                 device_id_type=MESH,
-            )
-
-        def start(step, carry):
-            copy_to(step).start()
+            ).start()
             return carry
 
-        def finish(step, carry):
-            sender = lax.rem(me + step, devices)
-            pltpu.make_async_remote_copy(
-                src_ref=source(sender),
-                dst_ref=target.at[sender],
-                send_sem=send_sem.at[phase, step],
-                recv_sem=recv_sem.at[phase, sender],
-                device_id=peer_of(step)[1],
-                device_id_type=MESH,
-            ).wait()
-            return carry
-
-        lax.fori_loop(1, devices, start, 0)
-        return lambda: lax.fori_loop(1, devices, finish, 0)
-
+        lax.fori_loop(1, devices, start, 0, unroll=True)
+
+        def finish():
+            every = target.at[pl.ds(0, devices - 1)]
+            pltpu.make_async_copy(every, every, send_sem.at[phase]).wait()
+            pltpu.make_async_copy(every, every, recv_sem.at[phase]).wait()
+
+        return finish
+
+    loads[0].wait()
     index_row = jnp.concatenate(
         [index_ref[...], jnp.zeros((1, LANES - own_active), jnp.int32)], axis=1
     )
@@ -109,6 +112,8 @@
     pl.semaphore_wait(barrier, devices - 1)
     finish_index = exchange(0, lambda peer: index_all.at[me], index_all)
 
+    for load in loads[1:]:
+        load.wait()
     piece = 1024
 
     def prepare(which, carry):
@@ -119,17 +124,17 @@
         mass, elapsed = mass_ref[:, at], time_ref[:, at]
         pred_pos, pred_vel = predict(old_pos, old_vel, old_acc, old_jerk, elapsed)
         rows = padded([old_pos, old_vel, old_acc, old_jerk, elapsed], 16)
-        packed[:, at] = padded(split3(rows), LANES).astype(BF16)
+        packed[:, at] = padded(split3(rows), DEEP).astype(BF16)
         field_pos[:, at] = padded([pred_pos], 8)
         moments = padded([mass * pred_pos, mass * pred_vel, mass], 8)
         split = jnp.concatenate(split3(moments), axis=0)
-        field_u[:, at] = padded([split], LANES).astype(BF16)
-        field_s[:, at] = padded([jnp.zeros((32, piece), F32), split], LANES).astype(BF16)
+        field_u[:, at] = padded([split], DEEP).astype(BF16)
+        field_s[:, at] = padded([jnp.zeros((32, piece), F32), split], DEEP).astype(BF16)
         pos_parts, vel_parts = split3(pred_pos), split3(pred_vel)
         dot_parts = split3(jnp.sum(pred_pos * pred_vel, axis=0, keepdims=True))
         ones = jnp.ones((1, piece), F32)
         rhs = [pos_parts[right] for _, right in PARTS] + [vel_parts[right] for _, right in PARTS]
-        motion_rhs[:, at] = padded(rhs + list(dot_parts) + [ones] * 3, LANES).astype(BF16)
+        motion_rhs[:, at] = padded(rhs + list(dot_parts) + [ones] * 3, DEEP).astype(BF16)
         return carry
 
     lax.fori_loop(0, own_stars // piece, prepare, 0)
@@ -148,7 +153,7 @@
     tile = min(ROWS, active)
 
     for block in range(active // tile):
-        picked[block * tile : (block + 1) * tile, :] = jnp.zeros((tile, LANES), F32)
+        picked[block * tile : (block + 1) * tile, :] = jnp.zeros((tile, DEEP), F32)
 
         def pick(which, carry):
             base = which * wide
@@ -189,7 +194,7 @@
         ones = jnp.ones((1, LANES), F32)
         lhs = [vel_parts[left] for left, _ in PARTS] + [pos_parts[left] for left, _ in PARTS]
         lhs = jnp.transpose(padded(lhs + [ones] * 3 + list(dot_parts), LANES))
-        rows_lhs[block * LANES : (block + 1) * LANES, :] = lhs.astype(BF16)
+        rows_lhs[block * LANES : (block + 1) * LANES, :] = lhs[:, :DEEP].astype(BF16)
         columns = jnp.transpose(padded([pred_pos], LANES))
         for axis in range(3):
             rows_pos[axis, block * LANES : (block + 1) * LANES, :] = jnp.broadcast_to(
@@ -228,13 +233,16 @@
         at = pl.ds(pl.multiple_of(which * CHUNK, CHUNK), CHUNK)
         near, far = field_u[:, at], field_s[:, at]
         field = jnp.concatenate([near, near, far, far], axis=1)
-        sums[pl.ds(first_row, tile), :] += lax.dot_general(
-            source[...], field, NT, preferred_element_type=F32
-        )
+        half = tile // 2
+        for part in range(2):
+            rows = pl.ds(first_row + part * half, half)
+            sums[rows, :] += lax.dot_general(
+                source[part * half : (part + 1) * half, :], field, NT, preferred_element_type=F32
+            )
 
     for block in range(active // tile):
         first_row = block * tile
-        sums[pl.ds(first_row, tile), :] = jnp.zeros((tile, LANES), F32)
+        sums[pl.ds(first_row, tile), :] = jnp.zeros((tile, DEEP), F32)
         pair_weights(first_row, 0, weights_a)
 
         def advance(which, carry):
@@ -272,10 +280,13 @@
     squared = elapsed * elapsed / 12.0
     new_vel = old_vel + 0.5 * elapsed * (old_acc + new_acc) + squared * (old_jerk - new_jerk)
     new_pos = old_pos + 0.5 * elapsed * (old_vel + new_vel) + squared * (old_acc - new_acc)
-    out_pos[...] = new_pos[:, :own_active]
-    out_vel[...] = new_vel[:, :own_active]
-    out_acc[...] = new_acc[:, :own_active]
-    out_jerk[...] = new_jerk[:, :own_active]
+    for number, value in enumerate((new_pos, new_vel, new_acc, new_jerk)):
+        result[number] = value[:, :own_active]
+
+
+def hand_out(result, out_pos, out_vel, out_acc, out_jerk):
+    for number, out in enumerate((out_pos, out_vel, out_acc, out_jerk)):
+        out[...] = result[number]
 
 
 def solution(mesh):
@@ -290,36 +301,44 @@
         tile = min(ROWS, active)
         out = jax.ShapeDtypeStruct((3, own_active), F32)
         vmem = pl.BlockSpec(memory_space=pltpu.VMEM)
-        return pl.pallas_call(
+        result = pl.pallas_call(
             functools.partial(kernel, blocks, groups, own_stars * devices),
-            out_shape=(out,) * 4,
-            in_specs=[vmem] * 7,
-            out_specs=(vmem,) * 4,
+            out_shape=jax.ShapeDtypeStruct((4, 3, own_active), F32),
+            in_specs=[pl.BlockSpec(memory_space=pltpu.HBM)] * 7,
+            out_specs=vmem,
             scratch_shapes=[
+                pltpu.VMEM((3, own_stars), F32),
+                pltpu.VMEM((3, own_stars), F32),
+                pltpu.VMEM((3, own_stars), F32),
+                pltpu.VMEM((3, own_stars), F32),
+                pltpu.VMEM((1, own_stars), F32),
+                pltpu.VMEM((1, own_stars), F32),
+                pltpu.VMEM((1, own_active), jnp.int32),
                 pltpu.VMEM((devices, 1, LANES), jnp.int32),
                 pltpu.VMEM((active, LANES), F32),
-                pltpu.VMEM((LANES, own_stars), BF16),
-                pltpu.VMEM((LANES, own_stars), BF16),
-                pltpu.VMEM((LANES, own_stars), BF16),
-                pltpu.VMEM((LANES, own_stars), BF16),
+                pltpu.VMEM((DEEP, own_stars), BF16),
+                pltpu.VMEM((DEEP, own_stars), BF16),
+                pltpu.VMEM((DEEP, own_stars), BF16),
+                pltpu.VMEM((DEEP, own_stars), BF16),
                 pltpu.VMEM((8, own_stars), F32),
-                pltpu.VMEM((active, LANES), F32),
+                pltpu.VMEM((active, DEEP), F32),
                 pltpu.VMEM((devices, 2, LANES), F32),
                 pltpu.VMEM((devices, 2, LANES), F32),
                 pltpu.VMEM((devices, 2, LANES), F32),
                 pltpu.VMEM((lane_blocks, 16, LANES), F32),
-                pltpu.VMEM((active, LANES), BF16),
+                pltpu.VMEM((active, DEEP), BF16),
                 pltpu.VMEM((3, active, LANES), F32),
                 pltpu.VMEM((tile, 4 * CHUNK), BF16),
                 pltpu.VMEM((tile, 4 * CHUNK), BF16),
-                pltpu.VMEM((active, LANES), F32),
+                pltpu.VMEM((active, DEEP), F32),
                 pltpu.VMEM((lane_blocks, 8, LANES), F32),
                 pltpu.VMEM((devices, 8, LANES), F32),
-                pltpu.SemaphoreType.DMA((4, devices)),
-                pltpu.SemaphoreType.DMA((4, devices)),
+                pltpu.SemaphoreType.DMA((4,)),
+                pltpu.SemaphoreType.DMA((4,)),
+                pltpu.SemaphoreType.DMA((7,)),
             ],
             compiler_params=pltpu.CompilerParams(
-                collective_id=0, has_side_effects=True, vmem_limit_bytes=40 * 1024 * 1024
+                collective_id=0, has_side_effects=True, vmem_limit_bytes=56 * 1024 * 1024
             ),
             cost_estimate=pl.CostEstimate(
                 flops=40 * active * own_stars, bytes_accessed=4 * 14 * own_stars,
@@ -330,6 +349,9 @@
             masses.reshape(1, own_stars), elapsed_time.reshape(1, own_stars),
             active_index.reshape(1, own_active),
         )
+        return pl.pallas_call(
+            hand_out, out_shape=(out,) * 4, in_specs=[vmem], out_specs=(vmem,) * 4
+        )(result)
 
     wide = P(None, ("blk", "group"))
     flat = P(("blk", "group"))

time: 65.1 us -> 56.5 us (0.87)
  local copies, waits for them, and re-layouts: 8.09 us -> 0 us
    unnamed x18 -> x0, local copies, waits for them, and re-layouts: 8.09 us -> none
    pallas_call x1, Pallas kernels: 56.1 us -> 54.3 us  [on_device(): pl.pallas_call(functools.partial(kernel, blocks, groups, own_stars * devi...]
    pallas_call x0 -> x1, Pallas kernels: none -> 1.29 us  [on_device(): pl.pallas_call(hand_out, out_shape=(out,) * 4, in_specs=[vmem], out_specs...]
where the time goes in v2:
time: 56.5 us; the launch traced here: 56.2 us
  Pallas kernels  55.6 us (98%)
  between operations  0.64 us (1%)
    pallas_call x1, Pallas kernels, on_device(): pl.pallas_call(functools.partial(kernel, blocks, groups, own_stars * devi...  54.3 us
    pallas_call x1, Pallas kernels, on_device(): pl.pallas_call(hand_out, out_shape=(out,) * 4, in_specs=[vmem], out_specs...  1.29 us

profile of v2, /device:TPU:0, one launch (start us, length us, event | category | flops | bytes accessed | tf_op | source)
XLA Modules:
  0.0 56.2 jit_solution(6097257879517925247)
XLA Ops:
  0.6 54.3 %shard_map.102.result = f32[4,3,16]{2,1,0:T(4,128)} custom-call(f32[3,8192]{1,0:T(4,128)} %pos_hbm.1, f32[3,8192]{1,0:T(4,128)} %vel_hbm.1, f32[3,8192]{1,0:T(4,128)} %acc_hbm.1, f32[3,8192]{1,0:T(4,128)} %jerk_hbm.1, f32[1,8192]{1,0:T(1,128)} %bitcast.3, f32[1,8192]{1,0:T(1,128)} %bitcast.4, s32[1,16]{1,0:T(1,128)} %bitcast.5), custom_call_target="tpu_custom_call" | custom-call | flops 167772160 | bytes 458752 | tf_op jit(solution)/shard_map/pallas_call | solution.py:304
  55.0 1.3 %shard_map.103 = (f32[3,16]{1,0:T(4,128)}, f32[3,16]{1,0:T(4,128)}, f32[3,16]{1,0:T(4,128)}, f32[3,16]{1,0:T(4,128)}) custom-call(f32[4,3,16]{2,1,0:T(4,128)} %shard_map.102.result), custom_call_target="tpu_custom_call" | custom-call | tf_op jit(solution)/shard_map/pallas_call | solution.py:352

commit v3 on v2

--- a/solution.py
+++ b/solution.py
@@ -12,11 +12,10 @@
 F32 = jnp.float32
 BF16 = jnp.bfloat16
 LANES = 128
-CHUNK = 512
+CHUNK = 256
 DEEP = 64
 ROWS = 512
 PARTS = ((0, 0), (0, 1), (1, 0), (0, 2), (2, 0), (1, 1))
-NT = (((1,), (1,)), ((), ()))
 
 
 def predict(pos_now, vel_now, acc_now, jerk_now, elapsed):
@@ -48,8 +47,8 @@
     pos_hbm, vel_hbm, acc_hbm, jerk_hbm, mass_hbm, time_hbm, index_hbm,
     result,
     pos_ref, vel_ref, acc_ref, jerk_ref, mass_ref, time_ref, index_ref,
-    index_all, index_col, packed, field_u, field_s, motion_rhs, field_pos,
-    picked, send_state, recv_state, state_all, state, rows_lhs, rows_pos,
+    index_all, packed, field, motion_lhs, star_pos,
+    picked, send_state, recv_state, state_all, state, rows_rhs, rows_pos,
     weights_a, weights_b, sums, send_force, recv_force,
     send_sem, recv_sem, load_sem,
 ):
@@ -108,7 +107,7 @@
     index_row = jnp.concatenate(
         [index_ref[...], jnp.zeros((1, LANES - own_active), jnp.int32)], axis=1
     )
-    index_all[me] = index_row
+    index_all[me] = pltpu.roll(index_row, own_active * lax.rem(me, per_block), 1)
     pl.semaphore_wait(barrier, devices - 1)
     finish_index = exchange(0, lambda peer: index_all.at[me], index_all)
 
@@ -125,56 +124,66 @@
         pred_pos, pred_vel = predict(old_pos, old_vel, old_acc, old_jerk, elapsed)
         rows = padded([old_pos, old_vel, old_acc, old_jerk, elapsed], 16)
         packed[:, at] = padded(split3(rows), DEEP).astype(BF16)
-        field_pos[:, at] = padded([pred_pos], 8)
         moments = padded([mass * pred_pos, mass * pred_vel, mass], 8)
-        split = jnp.concatenate(split3(moments), axis=0)
-        field_u[:, at] = padded([split], DEEP).astype(BF16)
-        field_s[:, at] = padded([jnp.zeros((32, piece), F32), split], DEEP).astype(BF16)
+        field[:, at] = padded(split3(moments), 32).astype(BF16)
         pos_parts, vel_parts = split3(pred_pos), split3(pred_vel)
         dot_parts = split3(jnp.sum(pred_pos * pred_vel, axis=0, keepdims=True))
         ones = jnp.ones((1, piece), F32)
-        rhs = [pos_parts[right] for _, right in PARTS] + [vel_parts[right] for _, right in PARTS]
-        motion_rhs[:, at] = padded(rhs + list(dot_parts) + [ones] * 3, DEEP).astype(BF16)
+        lhs = [pos_parts[right] for _, right in PARTS] + [vel_parts[right] for _, right in PARTS]
+        lhs = padded(lhs + list(dot_parts) + [ones] * 3, 48)
+        lhs = padded([lhs, pred_pos], DEEP)
+        for part in range(piece // LANES):
+            turned = jnp.transpose(lhs[:, part * LANES : (part + 1) * LANES])
+            down = pl.ds(pl.multiple_of(which * piece + part * LANES, LANES), LANES)
+            motion_lhs[down, :] = turned.astype(BF16)
+            for axis in range(3):
+                star_pos[axis, down, :] = jnp.broadcast_to(
+                    turned[:, 48 + axis : 49 + axis], (LANES, LANES)
+                )
         return carry
 
     lax.fori_loop(0, own_stars // piece, prepare, 0)
 
     finish_index()
     first = me * own_stars
-    local = (index_all[...].reshape(devices, LANES) - first).astype(F32)
-    local = jnp.transpose(local)
-    for device in range(devices):
-        column = local[:own_active, device : device + 1]
-        index_col[device * own_active : (device + 1) * own_active, :] = jnp.broadcast_to(
-            column, (own_active, LANES)
-        )
-
-    wide = 512
+    local = [
+        jnp.sum(index_all[block * per_block : (block + 1) * per_block], axis=0) - first
+        for block in range(lane_blocks)
+    ]
+
+    wide = 256
     tile = min(ROWS, active)
+    across = tile // LANES
+    down_16 = lax.broadcasted_iota(jnp.int32, (16, LANES), 0)
+    picked[...] = jnp.zeros((DEEP, active), F32)
 
     for block in range(active // tile):
-        picked[block * tile : (block + 1) * tile, :] = jnp.zeros((tile, DEEP), F32)
+        columns = slice(block * tile, (block + 1) * tile)
 
         def pick(which, carry):
             base = which * wide
             at = pl.ds(pl.multiple_of(base, wide), wide)
-            lanes = lax.broadcasted_iota(jnp.int32, (1, wide), 1) + base
-            lanes = lanes.astype(F32)
-            pieces = []
-            for part in range(wide // LANES):
-                column = index_col[block * tile : (block + 1) * tile, :]
-                same = column == lanes[:, part * LANES : (part + 1) * LANES]
-                pieces.append(jnp.where(same, 1.0, 0.0).astype(BF16))
-            chosen = jnp.concatenate(pieces, axis=1)
-            picked[block * tile : (block + 1) * tile, :] += lax.dot_general(
-                chosen, packed[:, at], NT, preferred_element_type=F32
+            mine = [local[block * across + part] - base for part in range(across)]
+            chosen = jnp.concatenate(
+                [
+                    jnp.concatenate(
+                        [
+                            jnp.where(down_16 == one - row, 1.0, 0.0).astype(BF16)
+                            for row in range(0, wide, 16)
+                        ],
+                        axis=0,
+                    )
+                    for one in mine
+                ],
+                axis=1,
             )
+            picked[:, columns] += jnp.dot(packed[:, at], chosen, preferred_element_type=F32)
             return carry
 
         lax.fori_loop(0, own_stars // wide, pick, 0)
 
     for block in range(lane_blocks):
-        turned = jnp.transpose(picked[block * LANES : (block + 1) * LANES, :])
+        turned = picked[:, block * LANES : (block + 1) * LANES]
         rows = turned[0:16] + turned[16:32] + turned[32:48]
         for pair in range(per_block):
             send_state[block * per_block + pair] = rows[2 * pair : 2 * pair + 2]
@@ -193,29 +202,33 @@
         dot_parts = split3(jnp.sum(pred_pos * pred_vel, axis=0, keepdims=True))
         ones = jnp.ones((1, LANES), F32)
         lhs = [vel_parts[left] for left, _ in PARTS] + [pos_parts[left] for left, _ in PARTS]
-        lhs = jnp.transpose(padded(lhs + [ones] * 3 + list(dot_parts), LANES))
-        rows_lhs[block * LANES : (block + 1) * LANES, :] = lhs[:, :DEEP].astype(BF16)
-        columns = jnp.transpose(padded([pred_pos], LANES))
-        for axis in range(3):
-            rows_pos[axis, block * LANES : (block + 1) * LANES, :] = jnp.broadcast_to(
-                columns[:, axis : axis + 1], (LANES, LANES)
-            )
+        lhs = padded(lhs + [ones] * 3 + list(dot_parts), DEEP)
+        rows_rhs[:, block * LANES : (block + 1) * LANES] = lhs.astype(BF16)
+        rows_pos[:, block * LANES : (block + 1) * LANES] = padded([pred_pos], 8)
 
     chunks = own_stars // CHUNK
 
     def pair_weights(first_row, which, target):
-        at = pl.ds(pl.multiple_of(which * CHUNK, CHUNK), CHUNK)
-        stars = [field_pos[axis : axis + 1, at] for axis in range(3)]
+        at = pl.multiple_of(which * CHUNK, CHUNK)
+        mine = [
+            [
+                rows_pos[axis : axis + 1, first_row + lane : first_row + lane + LANES]
+                for axis in range(3)
+            ]
+            for lane in range(0, tile, LANES)
+        ]
         along = jnp.dot(
-            rows_lhs[pl.ds(first_row, tile), :], motion_rhs[:, at], preferred_element_type=F32
+            motion_lhs[pl.ds(at, CHUNK), :],
+            rows_rhs[:, first_row : first_row + tile],
+            preferred_element_type=F32,
         )
         high = 16
-        for row in range(0, tile, high):
-            mine = [rows_pos[axis, pl.ds(first_row + row, high), :] for axis in range(3)]
-            for lane in range(0, CHUNK, LANES):
+        for row in range(0, CHUNK, high):
+            stars = [star_pos[axis, pl.ds(at + row, high), :] for axis in range(3)]
+            for lane in range(0, tile, LANES):
                 squares = []
                 for axis in range(3):
-                    offset = stars[axis][:, lane : lane + LANES] - mine[axis]
+                    offset = stars[axis] - mine[lane // LANES][axis]
                     squares.append(offset * offset)
                 inverse = lax.rsqrt(squares[0] + squares[1] + squares[2] + softening)
                 inverse_sq = inverse * inverse
@@ -224,25 +237,24 @@
                 for number, value in enumerate((cubed, slope)):
                     near = value.astype(BF16)
                     far = (value - near.astype(F32)).astype(BF16)
-                    start = 2 * number * CHUNK + lane
-                    target[row : row + high, start : start + LANES] = near
+                    start = 2 * number * CHUNK + row
+                    target[start : start + high, lane : lane + LANES] = near
                     start += CHUNK
-                    target[row : row + high, start : start + LANES] = far
+                    target[start : start + high, lane : lane + LANES] = far
 
     def add_up(first_row, which, source):
         at = pl.ds(pl.multiple_of(which * CHUNK, CHUNK), CHUNK)
-        near, far = field_u[:, at], field_s[:, at]
-        field = jnp.concatenate([near, near, far, far], axis=1)
-        half = tile // 2
-        for part in range(2):
-            rows = pl.ds(first_row + part * half, half)
-            sums[rows, :] += lax.dot_general(
-                source[part * half : (part + 1) * half, :], field, NT, preferred_element_type=F32
+        twice = jnp.concatenate([field[:, at]] * 2, axis=1)
+        for number in range(2):
+            sums[number, :, first_row : first_row + tile] += jnp.dot(
+                twice,
+                source[2 * number * CHUNK : 2 * (number + 1) * CHUNK, :],
+                preferred_element_type=F32,
             )
 
+    sums[...] = jnp.zeros((2, 32, active), F32)
     for block in range(active // tile):
         first_row = block * tile
-        sums[pl.ds(first_row, tile), :] = jnp.zeros((tile, DEEP), F32)
         pair_weights(first_row, 0, weights_a)
 
         def advance(which, carry):
@@ -256,9 +268,10 @@
 
     gravity = 1.0 / total_stars
     for block in range(lane_blocks):
-        turned = jnp.transpose(sums[block * LANES : (block + 1) * LANES, :])
+        turned = sums[0, :, block * LANES : (block + 1) * LANES]
         plain = turned[0:8] + turned[8:16] + turned[16:24]
-        sloped = turned[32:40] + turned[40:48] + turned[48:56]
+        turned = sums[1, :, block * LANES : (block + 1) * LANES]
+        sloped = turned[0:8] + turned[8:16] + turned[16:24]
         rows = state[block]
         pred_pos, pred_vel = predict(rows[0:3], rows[3:6], rows[6:9], rows[9:12], rows[12:13])
         accel = plain[0:3] - pred_pos * plain[6:7]
@@ -315,22 +328,20 @@
                 pltpu.VMEM((1, own_stars), F32),
                 pltpu.VMEM((1, own_active), jnp.int32),
                 pltpu.VMEM((devices, 1, LANES), jnp.int32),
-                pltpu.VMEM((active, LANES), F32),
                 pltpu.VMEM((DEEP, own_stars), BF16),
-                pltpu.VMEM((DEEP, own_stars), BF16),
-                pltpu.VMEM((DEEP, own_stars), BF16),
-                pltpu.VMEM((DEEP, own_stars), BF16),
-                pltpu.VMEM((8, own_stars), F32),
-                pltpu.VMEM((active, DEEP), F32),
+                pltpu.VMEM((32, own_stars), BF16),
+                pltpu.VMEM((own_stars, DEEP), BF16),
+                pltpu.VMEM((3, own_stars, LANES), F32),
+                pltpu.VMEM((DEEP, active), F32),
                 pltpu.VMEM((devices, 2, LANES), F32),
                 pltpu.VMEM((devices, 2, LANES), F32),
                 pltpu.VMEM((devices, 2, LANES), F32),
                 pltpu.VMEM((lane_blocks, 16, LANES), F32),
-                pltpu.VMEM((active, DEEP), BF16),
-                pltpu.VMEM((3, active, LANES), F32),
-                pltpu.VMEM((tile, 4 * CHUNK), BF16),
-                pltpu.VMEM((tile, 4 * CHUNK), BF16),
-                pltpu.VMEM((active, DEEP), F32),
+                pltpu.VMEM((DEEP, active), BF16),
+                pltpu.VMEM((8, active), F32),
+                pltpu.VMEM((4 * CHUNK, tile), BF16),
+                pltpu.VMEM((4 * CHUNK, tile), BF16),
+                pltpu.VMEM((2, 32, active), F32),
                 pltpu.VMEM((lane_blocks, 8, LANES), F32),
                 pltpu.VMEM((devices, 8, LANES), F32),
                 pltpu.SemaphoreType.DMA((4,)),

time: 56.5 us -> 50.8 us (0.90)
  Pallas kernels: 55.6 us -> 49.9 us
    pallas_call x1, Pallas kernels: 54.3 us -> 48.6 us  [on_device(): pl.pallas_call(functools.partial(kernel, blocks, groups, own_stars * devi...]
where the time goes in v3:
time: 50.8 us; the launch traced here: 50.6 us
  Pallas kernels  49.9 us (98%)
  between operations  0.64 us (1%)
    pallas_call x1, Pallas kernels, on_device(): pl.pallas_call(functools.partial(kernel, blocks, groups, own_stars * devi...  48.6 us
    pallas_call x1, Pallas kernels, on_device(): pl.pallas_call(hand_out, out_shape=(out,) * 4, in_specs=[vmem], out_specs...  1.29 us

profile of v3, /device:TPU:0, one launch (start us, length us, event | category | flops | bytes accessed | tf_op | source)
XLA Modules:
  0.0 50.6 jit_solution(1944612237034676292)
XLA Ops:
  0.6 48.6 %shard_map.102.result = f32[4,3,16]{2,1,0:T(4,128)} custom-call(f32[3,8192]{1,0:T(4,128)} %pos_hbm.1, f32[3,8192]{1,0:T(4,128)} %vel_hbm.1, f32[3,8192]{1,0:T(4,128)} %acc_hbm.1, f32[3,8192]{1,0:T(4,128)} %jerk_hbm.1, f32[1,8192]{1,0:T(1,128)} %bitcast.3, f32[1,8192]{1,0:T(1,128)} %bitcast.4, s32[1,16]{1,0:T(1,128)} %bitcast.5), custom_call_target="tpu_custom_call" | custom-call | flops 167772160 | bytes 458752 | tf_op jit(solution)/shard_map/pallas_call | solution.py:317
  49.3 1.3 %shard_map.103 = (f32[3,16]{1,0:T(4,128)}, f32[3,16]{1,0:T(4,128)}, f32[3,16]{1,0:T(4,128)}, f32[3,16]{1,0:T(4,128)}) custom-call(f32[4,3,16]{2,1,0:T(4,128)} %shard_map.102.result), custom_call_target="tpu_custom_call" | custom-call | tf_op jit(solution)/shard_map/pallas_call | solution.py:363
